TPU v7x, 256 devices: a whole 4x4x8 slice. The times are simulated.
256 devices in a mesh: patch: 64 (over x_lo, z, y), head: 4 (over x_hi, core).
Axes of the slice: x: 4 (x_hi: 2, x_lo: 2; x = x_hi * 2 + x_lo), y: 4, z: 8, core: 2. Of those that a mesh axis runs over, the one named last changes fastest.
Arguments:
- tokens: bfloat16 [12288, 3072], P('patch'), may hold values from -6 to 6
- valid_counts: int32 [64], replicated, may hold values from 96 to 192, as said below
- mod_shift: float32 [3072], replicated, may hold values from -3 to 3
- mod_scale: float32 [3072], replicated, may hold values from -3 to 3
- mod_gate: float32 [3072], P('head'), may hold values from 8 to 64
- q_gain: float32 [128], replicated, may hold values from 0.6 to 96
- w_qkv: bfloat16 [3072, 3, 1536], P('patch', None, 'head'), may hold values from -0.109375 to 0.109375
- w_out: bfloat16 [1536, 3072], P('head', 'patch'), may hold values from -0.15625 to 0.15625
- stale_keys: bfloat16 [12288, 1536], P('patch', 'head'), may hold values from -8 to 8
- stale_values: bfloat16 [12288, 1536], P('patch', 'head'), may hold values from -6 to 6
Outputs:
- mixed: bfloat16 [12288, 3072], P('patch', 'head')
Inputs may be any that keep to these rules, and one draw needn't show every extreme that they name: `valid_counts`: every slab has at least half of its slots real; some slab is full in every draw.
All inputs are finite; a program needn't handle non-finite values.
Results may differ from a plain program's by a relative error of at most 0.019.
Values may be sent and summed in bfloat16 or wider, within the bound.
A program may use at most 128 MiB of HBM per device.

v0:
```python
import math

import jax
import jax.numpy as jnp
from jax import lax
from jax.sharding import PartitionSpec as P

HEAD_DIM = 128


def head_norm(raw):
    return raw / jnp.sqrt(jnp.mean(raw * raw, axis=-1, keepdims=True) + 1e-06)


def key_validity(start, length, slab_rows, valid_counts):
    positions = start + jnp.arange(length, dtype=jnp.int32)
    slab_of = positions // slab_rows
    slot_of = positions % slab_rows
    slab_ids = jnp.arange(valid_counts.shape[0], dtype=jnp.int32)
    limits = jnp.sum(
        jnp.where(slab_of[:, None] == slab_ids[None, :], valid_counts[None, :], 0), axis=1
    )
    return (slot_of < limits, slab_of)


def attend_block(carry, queries, key_block, value_block, keep, score_scale):
    rowmax, total, numer = carry
    scores = (
        jnp.einsum("qhd,khd->hqk", queries, key_block, preferred_element_type=jnp.float32)
        * score_scale
    )
    scores = jnp.where(keep[None, None, :], scores, -jnp.inf)
    newmax = jnp.maximum(rowmax, jnp.max(scores, axis=2))
    factor = jnp.exp(rowmax - newmax)
    weights = jnp.exp(scores - newmax[:, :, None])
    total = total * factor + jnp.sum(weights, axis=2)
    numer = numer * factor[:, :, None] + jnp.einsum(
        "hqk,khd->hqd",
        weights.astype(jnp.bfloat16),
        value_block,
        preferred_element_type=jnp.float32,
    )
    return (newmax, total, numer)


def shards(
    tokens,
    valid_counts,
    mod_shift,
    mod_scale,
    mod_gate,
    q_gain,
    w_qkv,
    w_out,
    stale_keys,
    stale_values,
):
    slab_rows = tokens.shape[0]
    local_hq = w_out.shape[0]
    local_heads = local_hq // HEAD_DIM
    score_scale = 1.0 / HEAD_DIM**0.5
    values_f = tokens.astype(jnp.float32)
    mean = jnp.mean(values_f, axis=1, keepdims=True)
    centred = values_f - mean
    variance = jnp.mean(centred * centred, axis=1, keepdims=True)
    normed = centred / jnp.sqrt(variance + 1e-06)
    modulated = (normed * (1.0 + mod_scale) + mod_shift).astype(jnp.bfloat16)
    piece = lax.all_gather(w_qkv, "patch", axis=0, tiled=True)
    flat = piece.reshape(piece.shape[0], 3 * local_hq)
    qkv = jnp.dot(modulated, flat, preferred_element_type=jnp.float32)
    raw_queries = qkv[:, :local_hq].reshape(slab_rows, local_heads, HEAD_DIM)
    raw_keys = qkv[:, local_hq : 2 * local_hq].reshape(slab_rows, local_heads, HEAD_DIM)
    queries = (head_norm(raw_queries) * q_gain).astype(jnp.bfloat16)
    fresh_keys = head_norm(raw_keys).astype(jnp.bfloat16)
    fresh_values = (
        qkv[:, 2 * local_hq :].astype(jnp.bfloat16).reshape(slab_rows, local_heads, HEAD_DIM)
    )
    my_slab = lax.axis_index("patch")
    own_start = my_slab * slab_rows
    own_keep, own_slabs = key_validity(own_start, slab_rows, slab_rows, valid_counts)
    start_state = (
        jnp.full((local_heads, slab_rows), -jnp.inf, jnp.float32),
        jnp.zeros((local_heads, slab_rows), jnp.float32),
        jnp.zeros((local_heads, slab_rows, HEAD_DIM), jnp.float32),
    )
    fresh_state = attend_block(
        start_state, queries, fresh_keys, fresh_values, own_keep, score_scale
    )
    all_keys, all_values = (
        lax.all_gather(stale_keys, "patch", axis=0, tiled=True),
        lax.all_gather(stale_values, "patch", axis=0, tiled=True),
    )
    length = all_keys.shape[0]
    block = math.gcd(length, 1024)
    count = length // block
    key_blocks = all_keys.reshape(count, block, local_heads, HEAD_DIM)
    value_blocks = all_values.reshape(count, block, local_heads, HEAD_DIM)

    def one_block(state, inputs):
        key_block, value_block, offset = inputs
        keep, slabs = key_validity(offset, block, slab_rows, valid_counts)
        keep = jnp.logical_and(keep, slabs != my_slab)
        return (attend_block(state, queries, key_block, value_block, keep, score_scale), None)

    offsets = jnp.arange(count, dtype=jnp.int32) * block
    result, unused = lax.scan(one_block, fresh_state, (key_blocks, value_blocks, offsets))
    rowmax, total, numer = result
    attended = numer / total[:, :, None]
    attended = jnp.transpose(attended, (1, 0, 2)).reshape(slab_rows, local_hq).astype(jnp.bfloat16)
    partial_sums = jnp.dot(
        attended,
        lax.all_gather(w_out, "patch", axis=1, tiled=True),
        preferred_element_type=jnp.float32,
    )
    projected = lax.psum_scatter(
        partial_sums.astype(jnp.bfloat16), "head", scatter_dimension=1, tiled=True
    ).astype(jnp.float32)
    return (mod_gate * projected).astype(jnp.bfloat16)


def solution(mesh):
    in_specs = (
        P("patch", None),
        P(),
        P(),
        P(),
        P("head"),
        P(),
        P("patch", None, "head"),
        P("head", "patch"),
        P("patch", "head"),
        P("patch", "head"),
    )
    out_specs = P("patch", "head")
    return jax.shard_map(shards, mesh=mesh, in_specs=in_specs, out_specs=out_specs, check_vma=False)
```

profile of v0, /device:TPU:1, one launch (start us, length us, event | category | flops | bytes accessed | tf_op | source)
XLA Modules:
  0.0 1297.9 jit_solution(11703523010474439441)
XLA Ops:
  6.5 0.7 all-gather.5.cloned.1.call-update
  7.3 0.7 all-gather.7.cloned.1.call-update
  8.1 0.7 all-gather.9.cloned.1.call-update
  9.4 1.5 convert_reduce_fusion
  11.6 272.0 %all-gather.5.cloned.1.call-done = bf16[3072,3,384]{2,0,1:T(8,128)(2,1)} async-done(((bf16[48,3,384]{2,0,1:T(8,128)(2,1)}), bf16[3072,3,384]{2,0,1:T(8,128)(2,1)}) %all-gather.5.cloned.1.call-update) | async-done | bytes 7077904 | tf_op jit(solution)/shard_map/all_gather | solution.py:68
  283.6 10.3 copy.61
  293.9 5.5 fusion.34
  301.9 295.8 %all-gather.7.cloned.1.call-done = bf16[12288,384]{1,0:T(8,128)(2,1)} async-done(((bf16[192,384]{1,0:T(8,128)(2,1)}), bf16[12288,384]{1,0:T(8,128)(2,1)}) %all-gather.7.cloned.1.call-update) | async-done | bytes 9437200 | tf_op jit(solution)/shard_map/all_gather | solution.py:90
  597.7 24.5 %reshape.129 = bf16[12,1024,3,128]{3,2,1,0:T(4,128)(2,1)} reshape(bf16[12288,384]{1,0:T(8,128)(2,1)} %all-gather.7.cloned.1.call-done) | data formatting | bytes 18874368 | tf_op jit(solution)/shard_map/reshape | solution.py:96
  622.1 10.7 copy.72
  632.8 279.8 %all-gather.9.cloned.1.call-done = bf16[12288,384]{1,0:T(8,128)(2,1)} async-done(((bf16[192,384]{1,0:T(8,128)(2,1)}), bf16[12288,384]{1,0:T(8,128)(2,1)}) %all-gather.9.cloned.1.call-update) | async-done | bytes 9437200 | tf_op jit(solution)/shard_map/all_gather | solution.py:91
  912.6 24.5 %reshape.130 = bf16[12,1024,3,128]{3,2,1,0:T(4,128)(2,1)} reshape(bf16[12288,384]{1,0:T(8,128)(2,1)} %all-gather.9.cloned.1.call-done) | data formatting | bytes 18874368 | tf_op jit(solution)/shard_map/reshape | solution.py:97
  937.0 10.8 copy.74
  947.9 74.1 %while.16 = (s32[]{:T(128)}, f32[3,192]{1,0:T(4,128)S(1)}, f32[3,192]{1,0:T(4,128)S(1)}, f32[3,192,128]{2,1,0:T(8,128)S(1)}, s32[12]{0:T(128)S(1)}, /*index=5*/s...) while((s32[]{:T(128)}, f32[3,192]{1,0:T(4,128)S(1)}, ...), condition=%wide.region_11.12_spmd, body=%wide.region_7.11_spmd.sunk | while | flops 308847744 | bytes 9446789 | solution.py:106
  949.7 1.7 bitcast_reduce_fusion.2
  951.5 0.6 fusion.73
  952.1 1.9 fusion.74
  954.0 0.6 dynamic_slice.35
  955.9 1.7 bitcast_reduce_fusion.2
  957.6 0.6 fusion.73
  958.3 1.9 fusion.74
  960.2 0.6 dynamic_slice.35
  962.1 1.7 bitcast_reduce_fusion.2
  963.8 0.6 fusion.73
  964.5 1.9 fusion.74
  966.4 0.6 dynamic_slice.35
  968.3 1.7 bitcast_reduce_fusion.2
  970.0 0.6 fusion.73
  970.6 1.9 fusion.74
  972.6 0.6 dynamic_slice.35
  974.4 1.7 bitcast_reduce_fusion.2
  976.2 0.6 fusion.73
  976.8 1.9 fusion.74
  978.7 0.6 dynamic_slice.35
  980.6 1.7 bitcast_reduce_fusion.2
  982.3 0.6 fusion.73
  983.0 1.9 fusion.74
  984.9 0.6 dynamic_slice.35
  986.8 1.7 bitcast_reduce_fusion.2
  988.5 0.6 fusion.73
  989.2 1.9 fusion.74
  991.1 0.6 dynamic_slice.35
  993.0 1.7 bitcast_reduce_fusion.2
  994.7 0.6 fusion.73
  995.3 1.9 fusion.74
  997.3 0.6 dynamic_slice.35
  999.1 1.7 bitcast_reduce_fusion.2
  1000.9 0.6 fusion.73
  1001.5 1.9 fusion.74
  1003.4 0.6 dynamic_slice.35
  1005.3 1.7 bitcast_reduce_fusion.2
  1007.0 0.6 fusion.73
  1007.7 1.9 fusion.74
  1009.6 0.6 dynamic_slice.35
  1011.5 1.7 bitcast_reduce_fusion.2
  1013.2 0.6 fusion.73
  1013.9 1.9 fusion.74
  1017.7 1.7 bitcast_reduce_fusion.2
  1019.4 0.6 fusion.73
  1020.0 1.9 fusion.74
  1022.0 184.3 %all-gather.11.cloned.1.call-done = bf16[384,3072]{0,1:T(8,128)(2,1)} async-done(((bf16[384,48]{0,1:T(8,128)(2,1)}), bf16[384,3072]{0,1:T(8,128)(2,1)}) %all-gather.11.cloned.1.call-update) | async-done | bytes 2359312 | tf_op jit(solution)/shard_map/all_gather | solution.py:112
  1206.3 3.7 convolution_convert_fusion
  1210.0 79.6 %reduce-scatter.2.cloned.1.call-done = bf16[192,768]{1,0:T(8,128)(2,1)} async-done(((bf16[192,3072]{1,0:T(8,128)(2,1)}), bf16[192,768]{1,0:T(8,128)(2,1)}) %reduce-scatter.2.cloned.1.call-update) | async-done | bytes 294928 | tf_op jit(solution)/shard_map/reduce_scatter | solution.py:115
  1289.7 1.7 multiply_convert_fusion
  (115 shorter events, 20.5 us)
Async XLA Ops:
  6.5 4.4 copy-start
  6.5 4.8 copy-start.2
  6.5 4.9 copy-start.1
  6.5 277.1 %all-gather.5.cloned.1.call-start = ((), (), s32[]{:S(2)}) async-start(), calls=%async_computation.1 | async-start | bytes 7188480 | tf_op jit(solution)/shard_map/all_gather | solution.py:68
  7.3 590.4 %all-gather.7.cloned.1.call-start = ((), (), s32[]{:S(2)}) async-start(), calls=%async_computation.2 | async-start | bytes 9584640 | tf_op jit(solution)/shard_map/all_gather | solution.py:90
  8.0 904.5 %all-gather.9.cloned.1.call-start = ((), (), s32[]{:S(2)}) async-start(), calls=%async_computation.3 | async-start | bytes 9584640 | tf_op jit(solution)/shard_map/all_gather | solution.py:91
  8.7 1197.6 %all-gather.11.cloned.1.call-start = ((), (), s32[]{:S(2)}) async-start(), calls=%async_computation.4 | async-start | bytes 2396160 | tf_op jit(solution)/shard_map/all_gather | solution.py:112
  9.3 1280.4 %reduce-scatter.2.cloned.1.call-start = ((), (), s32[]{:S(2)}) async-start(), calls=%async_computation.5 | async-start | bytes 1474560 | tf_op jit(solution)/shard_map/reduce_scatter | solution.py:115
  11.5 282.3 %copy-start.5 = (f32[3072]{0:T(1024)S(1)}, f32[3072]{0:T(1024)}, u32[]{:S(2)}) copy-start(f32[3072]{0:T(1024)} %param.14) | copy-start | bytes 36868
  299.4 0.7 copy-start.4
  1206.3 83.4 %copy-start.3 = (f32[768]{0:T(1024)S(1)}, f32[768]{0:T(1024)}, u32[]{:S(2)}) copy-start(f32[768]{0:T(1024)} %param.16) | copy-start | bytes 9220
Sparse Core Ops, SparseCore 0:
  9.2 274.3 all-gather.4
  285.4 312.2 all-gather.6
  599.4 313.0 all-gather.8
  914.2 292.0 all-gather.10
  1210.2 79.4 reduce-scatter.1
where the time goes:
time: 1300 us
  waiting for transfers between devices  1110 us (85%)
  local copies, waits for them, and re-layouts  88.4 us (7%)
  matrix products  52.9 us (4%)
  other arithmetic  28.4 us (2%)
  between operations  13.3 us (1%)
    all_gather x1, waiting for transfers between devices, shards(): lax.all_gather(stale_keys, 'patch', axis=0, tiled=True)  296 us
    all_gather x1, waiting for transfers between devices, shards(): lax.all_gather(stale_values, 'patch', axis=0, tiled=True)  280 us
    all_gather x1, waiting for transfers between devices, shards(): piece = lax.all_gather(w_qkv, 'patch', axis=0, tiled=True)  272 us
    all_gather x1, waiting for transfers between devices, shards(): lax.all_gather(w_out, 'patch', axis=1, tiled=True)  184 us
    reduce_scatter x1, waiting for transfers between devices, shards(): lax.psum_scatter(partial_sums.astype(jnp.bfloat16), 'head', scatter_dimen...  79.6 us
  transfers between devices with their start and end apart: 5, of which 5 were waited for; matrix products, arithmetic and copies ran while one was open for 13% of the time, Pallas kernels for 0%

commit v1 on v0

v1 whole, which is shorter than its diff:
```python
import functools
import math

import jax
import jax.numpy as jnp
from jax import lax
from jax.experimental import pallas as pl
from jax.experimental.pallas import tpu as pltpu
from jax.sharding import PartitionSpec as P

MESH = pl.DeviceIdType.MESH
F32 = jnp.float32
BF16 = jnp.bfloat16
ROWS = 192
D = 3072
HQ = 384
HD = 128
NZ, NY, NX = 8, 4, 4
SHARD = 48
C2 = math.log2(math.e) / math.sqrt(HD)
NEG = -1e30
N_SEM = 104


def dev(x, z, y, c):
    return ((lax.rem(x, 2) * NZ + z) * NY + y, (x // 2) * 2 + c)


def kernel(counts, tokens, scale, shift, gain, gate, w_in, wo_in, k_in, v_in, out,
           tok, xmod, wbuf, kv, mask, qbuf, s_scr, stat, osend, orecv, att, wo, gbuf, mix,
           ssem, rsem):
    p = lax.axis_index("patch")
    h = lax.axis_index("head")
    xl, z, y = p // (NZ * NY), lax.rem(p // NY, NZ), lax.rem(p, NY)
    xh, c = h // 2, lax.rem(h, 2)
    x = xh * 2 + xl
    oc = 1 - c

    def zat(k):
        return lax.rem(z + k + NZ, NZ)

    def yat(k):
        return lax.rem(y + k + NY, NY)

    def xat(k):
        return lax.rem(x + k + NX, NX)

    def to_z(k):
        return dev(x, zat(k), y, c)

    def to_y(k):
        return dev(x, z, yat(k), c)

    sibling = dev(x, z, y, oc)
    stays = c == xl

    next_sem = [0]

    def new_sem():
        next_sem[0] += 1
        return next_sem[0] - 1

    class Link:
        def __init__(self, src, dst, target, landing=None):
            n = new_sem()
            self.send = pltpu.make_async_remote_copy(
                src_ref=src, dst_ref=dst, send_sem=ssem.at[n], recv_sem=rsem.at[n],
                device_id=target, device_id_type=MESH)
            land = dst if landing is None else landing
            self.recv = pltpu.make_async_remote_copy(
                src_ref=land, dst_ref=land, send_sem=ssem.at[n], recv_sem=rsem.at[n],
                device_id=target, device_id_type=MESH)
            self.n = n
            self.sent = False

        def start(self):
            self.send.start()
            return self

        def arrived(self):
            self.recv.wait_recv()

        def done(self):
            if not self.sent:
                self.send.wait_send()
                self.sent = True

    links = []

    def post(src, dst, target, landing=None):
        link = Link(src, dst, target, landing).start()
        links.append(link)
        return link

    barrier = pltpu.get_barrier_semaphore()
    for k in range(NX):
        for cc in range(2):
            if k == 0 and cc == 0:
                continue
            pl.semaphore_signal(barrier, inc=1, device_id=dev(xat(k), z, y, lax.rem(c + cc, 2)),
                                device_id_type=MESH)
    for k in range(1, NZ):
        pl.semaphore_signal(barrier, inc=1, device_id=to_z(k), device_id_type=MESH)
    for k in range(1, NY):
        pl.semaphore_signal(barrier, inc=1, device_id=to_y(k), device_id_type=MESH)
    pl.semaphore_wait(barrier, 2 * NX - 1 + NZ - 1 + NY - 1)

    partner = dev(xh * 2 + c, z, y, xl)

    class Swap:
        def __init__(self, src, here, there):
            n = new_sem()
            self.local = pltpu.make_async_copy(src, here, ssem.at[n])
            self.remote = pltpu.make_async_remote_copy(
                src_ref=src, dst_ref=there, send_sem=ssem.at[n], recv_sem=rsem.at[n],
                device_id=partner, device_id_type=MESH)
            self.landing = pltpu.make_async_remote_copy(
                src_ref=here, dst_ref=here, send_sem=ssem.at[n], recv_sem=rsem.at[n],
                device_id=partner, device_id_type=MESH)

        def start(self):
            @pl.when(stays)
            def _():
                self.local.start()

            @pl.when(jnp.logical_not(stays))
            def _():
                self.remote.start()
            return self

        def wait(self):
            @pl.when(stays)
            def _():
                self.local.wait()

            @pl.when(jnp.logical_not(stays))
            def _():
                self.remote.wait_send()
                self.landing.wait_recv()

    in_q = Swap(w_in.at[pl.ds(0, 1)], wbuf.at[pl.ds(0, 1), c, z, y], wbuf.at[pl.ds(0, 1), oc, z, y]).start()
    in_kv = Swap(w_in.at[pl.ds(1, 2)], wbuf.at[pl.ds(1, 2), c, z, y], wbuf.at[pl.ds(1, 2), oc, z, y]).start()

    half = ROWS // 2
    tok_sem = [new_sem(), new_sem()]
    tok_local = pltpu.make_async_copy(tokens, tok, ssem.at[tok_sem[0]])

    def tok_copy(k):
        rows = pl.ds(k * half, half)
        xo = xat(1 - 2 * k)
        return pltpu.make_async_remote_copy(
            src_ref=tokens.at[rows], dst_ref=tok.at[rows], send_sem=ssem.at[tok_sem[k]],
            recv_sem=rsem.at[tok_sem[k]], device_id=dev(xo, z, y, oc), device_id_type=MESH)

    @pl.when(stays)
    def _():
        tok_local.start()

    @pl.when(jnp.logical_not(stays))
    def _():
        tok_copy(0).start()
        tok_copy(1).start()

    in_k = Swap(k_in, kv.at[0, c, z], kv.at[0, oc, z]).start()
    in_v = Swap(v_in, kv.at[1, c, z], kv.at[1, oc, z]).start()
    in_g = Swap(gate, gbuf, gbuf).start()

    zh = z // 4
    wo_x, wo_c = 2 * xl + zh, xh
    wo_self = jnp.logical_and(wo_x == x, wo_c == c)
    wo_sem = [new_sem(), new_sem()]

    def wo_first(core):
        return pltpu.make_async_remote_copy(
            src_ref=wo_in, dst_ref=wo.at[h, lax.rem(z, 4), y], send_sem=ssem.at[wo_sem[core]],
            recv_sem=rsem.at[wo_sem[core]], device_id=dev(wo_x, z, y, wo_c), device_id_type=MESH)

    def wo_local(core):
        return pltpu.make_async_copy(wo_in, wo.at[h, lax.rem(z, 4), y], ssem.at[wo_sem[core]])

    for core in range(2):
        @pl.when(jnp.logical_and(c == core, wo_self))
        def _():
            wo_local(core).start()

        @pl.when(jnp.logical_and(c == core, jnp.logical_not(wo_self)))
        def _():
            wo_first(core).start()

    in_q.wait()
    wq_z = []
    for k in (1, -1, 2, -2, 3, -3, 4):
        wq_z.append(post(wbuf.at[0, c, z, y], wbuf.at[0, c, z, y], to_z(k),
                         landing=wbuf.at[0, c, zat(-k), y]))
    in_kv.wait()

    def ring(block, first, second):
        state = {}

        def step(s):
            if s > 0:
                for link in state[s - 1]:
                    link.arrived()
            if s > 3:
                return
            if s < 3:
                right = post(block(zat(-s)), block(zat(-s)), to_z(1), landing=block(zat(-1 - s)))
                left = post(block(zat(s)), block(zat(s)), to_z(-1), landing=block(zat(1 + s)))
            else:
                right = post(first(zat(-s)), first(zat(-s)), to_z(1), landing=first(zat(-1 - s)))
                left = post(second(zat(s)), second(zat(s)), to_z(-1), landing=second(zat(1 + s)))
            state[s] = (right, left)
        return step

    wkv_step = ring(lambda b: wbuf.at[pl.ds(1, 2), c, b, y],
                    lambda b: wbuf.at[pl.ds(1, 1), c, b, y],
                    lambda b: wbuf.at[pl.ds(2, 1), c, b, y])
    kv_ring = ring(lambda b: kv.at[:, c, b],
                   lambda b: kv.at[pl.ds(0, 1), c, b],
                   lambda b: kv.at[pl.ds(1, 1), c, b])
    kv_sib = []

    def kv_share(b):
        kv_sib.append(post(kv.at[:, c, b], kv.at[:, c, b], sibling, landing=kv.at[:, oc, b]))

    def kv_step(s):
        kv_ring(s)
        if s == 0:
            kv_share(z)
        elif s < 4:
            kv_share(zat(-s))
            kv_share(zat(s))
        else:
            kv_share(zat(4))

    def w_y(i):
        st = {}
        sib = []

        def share(b):
            sib.append(post(wbuf.at[i, c, :, b], wbuf.at[i, c, :, b], sibling,
                            landing=wbuf.at[i, oc, :, b]))

        def begin():
            src = wbuf.at[i, c, :, y]
            st["r"] = post(src, src, to_y(1), landing=wbuf.at[i, c, :, yat(-1)])
            st["l"] = post(src, src, to_y(-1), landing=wbuf.at[i, c, :, yat(1)])
            share(y)

        def middle():
            lo, hi = pl.ds(0, 4), pl.ds(4, 4)
            st["r"].arrived()
            src = wbuf.at[i, c, lo, yat(-1)]
            st["rr"] = post(src, src, to_y(1), landing=wbuf.at[i, c, lo, yat(2)])
            st["l"].arrived()
            src = wbuf.at[i, c, hi, yat(1)]
            st["ll"] = post(src, src, to_y(-1), landing=wbuf.at[i, c, hi, yat(2)])
            share(yat(-1))
            share(yat(1))

        def end():
            st["rr"].arrived()
            st["ll"].arrived()
            share(yat(2))

        def ready():
            for link in sib:
                link.arrived()
        return begin, middle, end, ready

    q_begin, q_middle, q_end, q_ready = w_y(0)
    k_begin, k_middle, k_end, k_ready = w_y(1)
    v_begin, v_middle, v_end, v_ready = w_y(2)

    wkv_step(0)

    rows_i = lax.broadcasted_iota(jnp.int32, (ROWS, HD), 0)
    lanes_i = lax.broadcasted_iota(jnp.int32, (ROWS, HD), 1)
    for s in range(16):
        limit = counts[s * NY + y]
        keep = jnp.logical_or(rows_i < limit, lanes_i > 0)
        mask[s] = jnp.where(keep, 0.0, NEG).astype(BF16)

    wkv_step(1)
    for link in wq_z:
        link.arrived()
    q_begin()
    in_k.wait()
    in_v.wait()
    kv_step(0)
    wkv_step(2)

    @pl.when(stays)
    def _():
        tok_local.wait()

    @pl.when(jnp.logical_not(stays))
    def _():
        tok_copy(0).wait()
        tok_copy(1).wait()

    def modulate(i, carry):
        r = pl.ds(pl.multiple_of(i * 16, 16), 16)
        t = tok[r, :].astype(F32)
        mean = jnp.mean(t, axis=1, keepdims=True)
        t = t - mean
        var = jnp.mean(t * t, axis=1, keepdims=True)
        t = t * lax.rsqrt(var + 1e-6)
        xmod[r, :] = (t * (1.0 + scale[...]) + shift[...]).astype(BF16)
        return carry

    lax.fori_loop(0, ROWS // 16, modulate, 0)
    wkv_step(3)
    q_middle()
    wkv_step(4)
    kv_step(1)
    q_end()
    k_begin()
    q_ready()

    def project(i):
        return jnp.dot(xmod[...], wbuf[i].reshape(D, HQ), preferred_element_type=F32)

    def head_norm(r):
        return r / jnp.sqrt(jnp.mean(r * r, axis=1, keepdims=True) + 1e-6)

    raw = project(0)
    for j in range(3):
        cols = slice(j * HD, (j + 1) * HD)
        qbuf[y, :, cols] = (head_norm(raw[:, cols]) * gain[...]).astype(BF16)
    q_links = {}
    for d in (1, 3, 2):
        q_links[d] = post(qbuf.at[y], qbuf.at[y], to_y(d), landing=qbuf.at[yat(-d)])
    kv_step(2)
    k_middle()
    v_begin()

    holds = zh == xl
    wo_rows = pl.ds(2 * c, 2)
    for core in range(2):
        from_self = jnp.logical_and(wo_self, c == core)

        @pl.when(from_self)
        def _():
            wo_local(core).wait()

        @pl.when(jnp.logical_and(holds, jnp.logical_not(from_self)))
        def _():
            wo_first(core).wait_recv()

        @pl.when(jnp.logical_and(c == core, jnp.logical_not(wo_self)))
        def _():
            wo_first(core).wait_send()

    woz_sem = [new_sem() for _ in range(7)]

    def woz(k, n):
        blk = wo.at[wo_rows, lax.rem(z, 4), y]
        return pltpu.make_async_remote_copy(
            src_ref=blk, dst_ref=blk, send_sem=ssem.at[woz_sem[n]], recv_sem=rsem.at[woz_sem[n]],
            device_id=to_z(k), device_id_type=MESH)

    def woz_landing(k, n):
        blk = wo.at[wo_rows, lax.rem(zat(-k), 4), y]
        return pltpu.make_async_remote_copy(
            src_ref=blk, dst_ref=blk, send_sem=ssem.at[woz_sem[n]], recv_sem=rsem.at[woz_sem[n]],
            device_id=to_z(k), device_id_type=MESH)

    zks = (1, -1, 2, -2, 3, -3, 4)
    kv_step(3)

    @pl.when(holds)
    def _():
        for n, k in enumerate(zks):
            woz(k, n).start()

    kv_step(4)
    for link in kv_sib:
        link.arrived()

    ones = jnp.ones((768, HD), BF16)

    def attend(yq, j):
        cols = pl.ds(pl.multiple_of(j * HD, HD), HD)
        first = (lax.broadcasted_iota(jnp.int32, (ROWS, HD), 1) == 0)
        q = jnp.concatenate([qbuf[yq, :, cols], jnp.where(first, 1.0, 0.0).astype(BF16)], axis=1)
        top = None
        for b in range(4):
            cc, zz = b // 2, 4 * (b % 2)
            kb = kv[0, cc, zz:zz + 4, :, cols].reshape(768, HD)
            mb = mask[4 * b:4 * b + 4].reshape(768, HD)
            kb = jnp.concatenate([kb, mb], axis=1)
            s = lax.dot_general(q, kb, (((1,), (1,)), ((), ())), preferred_element_type=F32)
            s_scr[:, 768 * b:768 * (b + 1)] = s
            for t in range(6):
                piece = s[:, t * HD:(t + 1) * HD]
                top = piece if top is None else jnp.maximum(top, piece)
        m = jnp.max(top, axis=1, keepdims=True)
        acc = jnp.zeros((ROWS, 2 * HD), F32)
        for b in range(4):
            cc, zz = b // 2, 4 * (b % 2)
            w = jnp.exp2((s_scr[:, 768 * b:768 * (b + 1)] - m) * C2).astype(BF16)
            vb = jnp.concatenate([kv[1, cc, zz:zz + 4, :, cols].reshape(768, HD), ones], axis=1)
            acc = acc + jnp.dot(w, vb, preferred_element_type=F32)
        total = acc[:, HD:]
        o = acc[:, :HD] / total
        return o, m * C2 + jnp.log2(total)

    def partial(d):
        def one(j, carry):
            o, lse = attend(yat(d), j)
            osend[d, :, pl.ds(pl.multiple_of(j * HD, HD), HD)] = o.astype(BF16)
            lane = lax.broadcasted_iota(jnp.int32, (ROWS, HD), 1)
            stat[...] = jnp.where(lane % 4 == j, lse, stat[...])
            return carry

        stat[...] = jnp.zeros_like(stat)
        lax.fori_loop(0, 3, one, 0)
        lane = lax.broadcasted_iota(jnp.int32, (ROWS, HD), 1)
        full = stat[...]
        top = full.astype(BF16).astype(F32)
        mid = (full - top).astype(BF16).astype(F32)
        low = full - top - mid
        osend[d, :, HQ:] = jnp.where(lane < 4, top, jnp.where(lane < 8, mid, low)).astype(BF16)
        return post(osend.at[d], orecv.at[d], to_y(d), landing=orecv.at[d])

    o_links = []
    q_links[3].arrived()
    o_links.append(partial(1))
    k_end()
    v_middle()
    k_ready()
    raw = project(1)
    fresh_k = [head_norm(raw[:, j * HD:(j + 1) * HD]).astype(BF16) for j in range(3)]
    for j in range(3):
        mix[:, j * HD:(j + 1) * HD] = fresh_k[j]
    q_links[1].arrived()
    o_links.append(partial(3))
    v_end()

    for n, k in enumerate(zks):
        src_holds = (zat(-k) // 4) == xl

        @pl.when(src_holds)
        def _():
            woz_landing(k, n).wait_recv()

        @pl.when(holds)
        def _():
            woz(k, n).wait_send()
    blk = wo.at[wo_rows, :, y]
    wo_r = post(blk, blk, to_y(1), landing=wo.at[wo_rows, :, yat(-1)])
    wo_l = post(blk, blk, to_y(-1), landing=wo.at[wo_rows, :, yat(1)])
    v_ready()
    raw = project(2)
    mix[:, HQ:] = raw.astype(BF16)
    q_links[2].arrived()
    o_links.append(partial(2))

    wo_r.arrived()
    blk = wo.at[wo_rows, pl.ds(0, 2), yat(-1)]
    wo_rr = post(blk, blk, to_y(1), landing=wo.at[wo_rows, pl.ds(0, 2), yat(2)])
    wo_l.arrived()
    blk = wo.at[wo_rows, pl.ds(2, 2), yat(1)]
    wo_ll = post(blk, blk, to_y(-1), landing=wo.at[wo_rows, pl.ds(2, 2), yat(2)])

    for link in links:
        if link not in o_links and link is not wo_rr and link is not wo_ll:
            link.done()
    kv[0, c, z] = mix[:, :HQ]
    kv[1, c, z] = mix[:, HQ:]

    for link in o_links:
        link.arrived()
    att_links = []
    for j in range(3):
        cols = slice(j * HD, (j + 1) * HD)
        own, own_lse = attend(y, j)
        lane = lax.broadcasted_iota(jnp.int32, (ROWS, HD), 1)
        parts, lses = [own], [own_lse[:, :1]]
        for d in (1, 3, 2):
            parts.append(orecv[d, :, cols].astype(F32))
            st = jnp.where(jnp.logical_and(lane % 4 == j, lane < 12), orecv[d, :, HQ:].astype(F32), 0.0)
            lses.append(jnp.sum(st, axis=1, keepdims=True))
        top = functools.reduce(jnp.maximum, lses)
        ws = [jnp.exp2(v - top) for v in lses]
        total = functools.reduce(jnp.add, ws)
        mixd = functools.reduce(jnp.add, [w * o for w, o in zip(ws, parts)])
        att[x, :, cols] = (mixd / total).astype(BF16)
        for k in (1, 3, 2):
            att_links.append(post(att.at[x, :, pl.ds(j * HD, HD)], att.at[x, :, pl.ds(j * HD, HD)],
                                  dev(xat(k), z, y, c),
                                  landing=att.at[xat(-k), :, pl.ds(j * HD, HD)]))
    wo_rr.arrived()
    wo_ll.arrived()
    blk = wo.at[wo_rows]
    wo_s = post(blk, blk, sibling, landing=wo.at[pl.ds(2 * oc, 2)])
    wo_s.arrived()
    for link in att_links:
        link.arrived()
    in_g.wait()
    acc = jnp.zeros((ROWS, 768), F32)
    for g in range(NX):
        acc = acc + lax.dot_general(att[g], wo[g].reshape(768, HQ), (((1,), (1,)), ((), ())),
                                    preferred_element_type=F32)
    mix[...] = (acc * gbuf[...]).astype(BF16)
    last = Swap(mix, out, out).start()
    last.wait()
    for link in links:
        link.done()
    assert next_sem[0] <= N_SEM, next_sem[0]


def shards(tokens, valid_counts, mod_shift, mod_scale, mod_gate, q_gain, w_qkv, w_out,
           stale_keys, stale_values):
    vm = pl.BlockSpec(memory_space=pltpu.VMEM)
    hbm = pl.BlockSpec(memory_space=pl.ANY)
    return pl.pallas_call(
        kernel,
        out_shape=jax.ShapeDtypeStruct((ROWS, 768), BF16),
        in_specs=[pl.BlockSpec(memory_space=pltpu.SMEM), hbm, vm, vm, vm, hbm, hbm, hbm, hbm, hbm],
        out_specs=hbm,
        scratch_shapes=[
            pltpu.VMEM((ROWS, D), BF16),
            pltpu.VMEM((ROWS, D), BF16),
            pltpu.VMEM((3, 2, NZ, NY, SHARD, HQ), BF16),
            pltpu.VMEM((2, 2, NZ, ROWS, HQ), BF16),
            pltpu.VMEM((16, ROWS, HD), BF16),
            pltpu.VMEM((NY, ROWS, HQ), BF16),
            pltpu.VMEM((ROWS, 16 * ROWS), F32),
            pltpu.VMEM((ROWS, HD), F32),
            pltpu.VMEM((NY, ROWS, HQ + HD), BF16),
            pltpu.VMEM((NY, ROWS, HQ + HD), BF16),
            pltpu.VMEM((NX, ROWS, HQ), BF16),
            pltpu.VMEM((4, 4, NY, SHARD, HQ), BF16),
            pltpu.VMEM((1, 768), F32),
            pltpu.VMEM((ROWS, 768), BF16),
            pltpu.SemaphoreType.DMA((N_SEM,)),
            pltpu.SemaphoreType.DMA((N_SEM,)),
        ],
        compiler_params=pltpu.CompilerParams(
            collective_id=0, has_side_effects=True, vmem_limit_bytes=48 * 2**20),
    )(valid_counts, tokens, mod_scale.reshape(1, D), mod_shift.reshape(1, D),
      q_gain.reshape(1, HD), mod_gate.reshape(1, 768), jnp.transpose(w_qkv, (1, 0, 2)),
      jnp.transpose(w_out), stale_keys, stale_values)


def solution(mesh):
    in_specs = (
        P("patch", None), P(), P(), P(), P("head"), P(), P("patch", None, "head"),
        P("head", "patch"), P("patch", "head"), P("patch", "head"),
    )
    return jax.shard_map(shards, mesh=mesh, in_specs=in_specs, out_specs=P("patch", "head"),
                         check_vma=False)
```

time: 1300 us -> 116 us (0.09)
  waiting for transfers between devices: 1110 us -> 0 us
  Pallas kernels: 0 us -> 107 us
  local copies, waits for them, and re-layouts: 88.4 us -> 8.88 us
  matrix products: 52.9 us -> 0 us
  other arithmetic: 28.4 us -> 0 us
  between operations: 13.3 us -> 0.02 us
    all_gather x4 -> x0, waiting for transfers between devices: 1030 us -> none  [the longest x1 296 us: shards(): lax.all_gather(stale_keys, 'patch', axis=0, tiled=True)]
    pallas_call x0 -> x1, Pallas kernels: none -> 107 us  [shards(): pl.pallas_call(kernel, out_shape=jax.ShapeDtypeStruct((ROWS, 768), BF16),...]
    reduce_scatter x1 -> x0, waiting for transfers between devices: 79.6 us -> none  [shards(): lax.psum_scatter(partial_sums.astype(jnp.bfloat16), 'head', scatter_dimen...]
    dot_general x28 -> x0, matrix products: 52.9 us -> none  [the longest x13 23 us: attend_block(): jnp.einsum('hqk,khd->hqd', weights.astype(jnp.bfloat16), value_block, pre...]
    reshape x4 -> x1, local copies, waits for them, and re-layouts: 49.2 us -> 0.69 us  [shards(): mod_gate.reshape(1, 768)]
    while x14 -> x0, local copies, waits for them, and re-layouts: 21.5 us -> none  [the longest x2 21.5 us: shards(): lax.scan(one_block, fresh_state, (key_blocks, value_blocks, offsets))]
  transfers between devices with their start and end apart: 5 -> 0, of which waited for: 5 -> 0; matrix products, arithmetic and copies ran while one was open for 13% -> 0% of each run, Pallas kernels for 0% -> 0%
where the time goes in v1:
time: 116 us
  Pallas kernels  107 us (92%)
  local copies, waits for them, and re-layouts  8.88 us (8%)
    pallas_call x1, Pallas kernels, shards(): pl.pallas_call(kernel, out_shape=jax.ShapeDtypeStruct((ROWS, 768), BF16),...  107 us
    unnamed x19, local copies, waits for them, and re-layouts  8.19 us

profile of v1, /device:TPU:1, one launch (start us, length us, event | category | flops | bytes accessed | tf_op | source)
XLA Modules:
  0.0 115.8 jit_solution(3435032483787276137)
XLA Ops:
  0.0 0.7 reshape.15.gate
  0.7 0.0 copy-start
  0.7 1.3 %copy-done = bf16[192,3072]{1,0:T(8,128)(2,1)S(1)} copy-done((bf16[192,3072]{1,0:T(8,128)(2,1)S(1)}, bf16[192,3072]{1,0:T(8,128)(2,1)}, u32[]{:S(2)}) %copy-start) | copy-done | bytes 1179672
  2.0 0.0 copy-start.1
  2.0 0.9 copy-done.1
  2.9 0.0 copy-start.2
  2.9 0.9 copy-done.2
  3.8 0.0 copy-start.3
  3.8 0.9 copy-done.3
  4.7 0.0 copy-start.4
  4.7 0.8 copy-done.4
  5.4 0.0 copy-start.5
  5.5 0.7 copy-done.5
  6.2 0.0 copy-start.6
  6.2 0.7 copy-done.6
  6.9 0.0 copy-start.7
  6.9 0.7 copy-done.7
  7.5 0.0 copy-start.8
  7.5 0.7 copy-done.8
  8.2 106.9 %shard_map.100 = bf16[192,768]{1,0:T(8,128)(2,1)S(1)} custom-call(s32[64]{0:T(128)S(1)} %copy-done.7, bf16[192,3072]{1,0:T(8,128)(2,1)S(1)} %copy-done, f32[1,3072]{1,0:T(1,128)S(1)} %bitcast.7, f32[1,3072]{1,0:T(1,128)S(1)} %bitcast.8, f32[1,128]{1,0:T(1,128)S(1)} %bitcast.9, f32[1,768]{1,0:T(1,128)S(1)} %reshape.15.gate, bf16[3,48,384]{2,1,0:T(8,128)(2,1)S(1)} %bitcast.5, ...), custom_call_target="tpu_custom_call" | custom-call | tf_op jit(solution)/shard_map/pallas_call | solution.py:518
  115.1 0.7 copy.12
Async XLA Ops:
  0.7 1.3 %copy-start = (bf16[192,3072]{1,0:T(8,128)(2,1)S(1)}, bf16[192,3072]{1,0:T(8,128)(2,1)}, u32[]{:S(2)}) copy-start(bf16[192,3072]{1,0:T(8,128)(2,1)} %tokens.1) | copy-start | bytes 3538948
  2.0 0.9 copy-start.1
  2.9 0.9 copy-start.2
  3.8 0.9 copy-start.3
  4.7 0.8 copy-start.4
  5.4 0.7 copy-start.5
  6.2 0.7 copy-start.6
  6.9 0.7 copy-start.7
  7.5 0.7 copy-start.8

commit v2 on v1

v2 whole, which is shorter than its diff:
```python
import functools
import math

import jax
import jax.numpy as jnp
from jax import lax
from jax.experimental import pallas as pl
from jax.experimental.pallas import tpu as pltpu
from jax.sharding import PartitionSpec as P

MESH = pl.DeviceIdType.MESH
F32 = jnp.float32
BF16 = jnp.bfloat16
ROWS = 192
D = 3072
HQ = 384
HD = 128
NZ, NY, NX = 8, 4, 4
SHARD = 48
C2 = math.log2(math.e) / math.sqrt(HD)
NEG = -1e30
N_SEM = 112


def dev(x, z, y, c):
    return ((lax.rem(x, 2) * NZ + z) * NY + y, (x // 2) * 2 + c)


def kernel(counts, tokens, scale_in, shift_in, gain_in, gate, w_in, wo_in, k_in, v_in, out,
           tok, scale, shift, gain, xmod, wbuf, kv, mask, qbuf, stat, osend, orecv, att, wo, gbuf, mix,
           run_m, run_acc, ssem, rsem):
    p = lax.axis_index("patch")
    h = lax.axis_index("head")
    xl, z, y = p // (NZ * NY), lax.rem(p // NY, NZ), lax.rem(p, NY)
    xh, c = h // 2, lax.rem(h, 2)
    x = xh * 2 + xl
    oc = 1 - c

    def zat(k):
        return lax.rem(z + k + NZ, NZ)

    def yat(k):
        return lax.rem(y + k + NY, NY)

    def xat(k):
        return lax.rem(x + k + NX, NX)

    def to_z(k):
        return dev(x, zat(k), y, c)

    def to_y(k):
        return dev(x, z, yat(k), c)

    sibling = dev(x, z, y, oc)
    stays = c == xl

    next_sem = [0]

    def new_sem():
        next_sem[0] += 1
        return next_sem[0] - 1

    class Link:
        def __init__(self, src, dst, target, landing=None):
            n = new_sem()
            self.send = pltpu.make_async_remote_copy(
                src_ref=src, dst_ref=dst, send_sem=ssem.at[n], recv_sem=rsem.at[n],
                device_id=target, device_id_type=MESH)
            land = dst if landing is None else landing
            self.recv = pltpu.make_async_remote_copy(
                src_ref=land, dst_ref=land, send_sem=ssem.at[n], recv_sem=rsem.at[n],
                device_id=target, device_id_type=MESH)
            self.n = n
            self.sent = False

        def start(self):
            self.send.start()
            return self

        def arrived(self):
            self.recv.wait_recv()

        def done(self):
            if not self.sent:
                self.send.wait_send()
                self.sent = True

    links = []

    def post(src, dst, target, landing=None):
        link = Link(src, dst, target, landing).start()
        links.append(link)
        return link

    small = [pltpu.make_async_copy(a, b, ssem.at[new_sem()])
             for a, b in ((scale_in, scale), (shift_in, shift), (gain_in, gain))]
    for copy in small:
        copy.start()

    barrier = pltpu.get_barrier_semaphore()
    for k in range(NX):
        for cc in range(2):
            if k == 0 and cc == 0:
                continue
            pl.semaphore_signal(barrier, inc=1, device_id=dev(xat(k), z, y, lax.rem(c + cc, 2)),
                                device_id_type=MESH)
    for k in range(1, NZ):
        pl.semaphore_signal(barrier, inc=1, device_id=to_z(k), device_id_type=MESH)
    for k in range(1, NY):
        pl.semaphore_signal(barrier, inc=1, device_id=to_y(k), device_id_type=MESH)

    @pl.when(z // 4 != xl)
    def _():
        pl.semaphore_signal(barrier, inc=1, device_id=dev(2 * c + xh, zat(4), y, 1), device_id_type=MESH)

    pl.semaphore_wait(barrier, 2 * NX - 1 + NZ - 1 + NY - 1 + c)

    partner = dev(xh * 2 + c, z, y, xl)

    class Swap:
        def __init__(self, src, here, there):
            n = new_sem()
            self.local = pltpu.make_async_copy(src, here, ssem.at[n])
            self.remote = pltpu.make_async_remote_copy(
                src_ref=src, dst_ref=there, send_sem=ssem.at[n], recv_sem=rsem.at[n],
                device_id=partner, device_id_type=MESH)
            self.landing = pltpu.make_async_remote_copy(
                src_ref=here, dst_ref=here, send_sem=ssem.at[n], recv_sem=rsem.at[n],
                device_id=partner, device_id_type=MESH)

        def start(self):
            @pl.when(stays)
            def _():
                self.local.start()

            @pl.when(jnp.logical_not(stays))
            def _():
                self.remote.start()
            return self

        def wait(self):
            @pl.when(stays)
            def _():
                self.local.wait()

            @pl.when(jnp.logical_not(stays))
            def _():
                self.remote.wait_send()
                self.landing.wait_recv()

    in_q = Swap(w_in.at[pl.ds(0, 1)], wbuf.at[pl.ds(0, 1), c, z, y], wbuf.at[pl.ds(0, 1), oc, z, y]).start()
    in_k = Swap(k_in, kv.at[0, c, z], kv.at[0, oc, z]).start()
    in_v = Swap(v_in, kv.at[1, c, z], kv.at[1, oc, z]).start()
    in_kv = Swap(w_in.at[pl.ds(1, 2)], wbuf.at[pl.ds(1, 2), c, z, y], wbuf.at[pl.ds(1, 2), oc, z, y]).start()

    wo_x, wo_c = 2 * xl + z // 4, xh
    wo_self = jnp.logical_and(jnp.logical_and(wo_x == x, wo_c == c), c == 0)
    wo_sem = new_sem()

    def wo_blk(zz, ys):
        group = 2 * c + jnp.where(zz // 4 == xl, 0, 1)
        return wo.at[group, lax.rem(zz, 4), ys]

    def wo_first(landing):
        dst = wo.at[h, lax.rem(z, 4), y]
        if landing:
            dst = wo_blk(z, y)
        return pltpu.make_async_remote_copy(
            src_ref=wo_in, dst_ref=dst, send_sem=ssem.at[wo_sem], recv_sem=rsem.at[wo_sem],
            device_id=dev(wo_x, lax.rem(z + 4 * c, NZ), y, wo_c), device_id_type=MESH)

    wo_local = pltpu.make_async_copy(wo_in, wo.at[h, lax.rem(z, 4), y], ssem.at[wo_sem])

    @pl.when(wo_self)
    def _():
        wo_local.start()

    @pl.when(jnp.logical_not(wo_self))
    def _():
        wo_first(False).start()

    tok_sem = [new_sem(), new_sem()]
    tok_local = pltpu.make_async_copy(tokens, tok, ssem.at[tok_sem[0]])

    def tok_copy(k):
        rows = pl.ds(0, 64) if k == 0 else pl.ds(64, 128)
        xo = x + 1 - 2 * xl if k == 0 else lax.rem(x + 3 + 2 * xl, NX)
        return pltpu.make_async_remote_copy(
            src_ref=tokens.at[rows], dst_ref=tok.at[rows], send_sem=ssem.at[tok_sem[k]],
            recv_sem=rsem.at[tok_sem[k]], device_id=dev(xo, z, y, oc), device_id_type=MESH)

    @pl.when(stays)
    def _():
        tok_local.start()

    @pl.when(jnp.logical_not(stays))
    def _():
        tok_copy(0).start()
        tok_copy(1).start()

    in_g = Swap(gate, gbuf, gbuf).start()

    in_q.wait()
    wq_z = []
    for k in (1, -1, 2, -2, 3, -3, 4):
        wq_z.append(post(wbuf.at[0, c, z, y], wbuf.at[0, c, z, y], to_z(k),
                         landing=wbuf.at[0, c, zat(-k), y]))

    def ring(block, first, second):
        state = {}

        def step(s):
            if s > 0:
                for link in state[s - 1]:
                    link.arrived()
            if s > 3:
                return
            if s < 3:
                right = post(block(zat(-s)), block(zat(-s)), to_z(1), landing=block(zat(-1 - s)))
                left = post(block(zat(s)), block(zat(s)), to_z(-1), landing=block(zat(1 + s)))
            else:
                right = post(first(zat(-s)), first(zat(-s)), to_z(1), landing=first(zat(-1 - s)))
                left = post(second(zat(s)), second(zat(s)), to_z(-1), landing=second(zat(1 + s)))
            state[s] = (right, left)
        return step, state

    wkv_step, _ = ring(lambda b: wbuf.at[pl.ds(1, 2), c, b, y],
                    lambda b: wbuf.at[pl.ds(1, 1), c, b, y],
                    lambda b: wbuf.at[pl.ds(2, 1), c, b, y])
    kv_ring, kv_state = ring(lambda b: kv.at[:, c, b],
                   lambda b: kv.at[pl.ds(0, 1), c, b],
                   lambda b: kv.at[pl.ds(1, 1), c, b])
    kv_sib = []

    def kv_share(b):
        kv_sib.append(post(kv.at[:, c, b], kv.at[:, c, b], sibling, landing=kv.at[:, oc, b]))

    def kv_step(s):
        kv_ring(s)
        if s == 0:
            kv_share(z)
        elif s < 4:
            kv_share(zat(-s))
            kv_share(zat(s))
        else:
            kv_share(zat(4))

    def w_y(i):
        st = {}
        sib = []

        def share(b):
            sib.append(post(wbuf.at[i, c, :, b], wbuf.at[i, c, :, b], sibling,
                            landing=wbuf.at[i, oc, :, b]))

        def begin():
            src = wbuf.at[i, c, :, y]
            st["r"] = post(src, src, to_y(1), landing=wbuf.at[i, c, :, yat(-1)])
            st["l"] = post(src, src, to_y(-1), landing=wbuf.at[i, c, :, yat(1)])
            share(y)

        def middle():
            lo, hi = pl.ds(0, 4), pl.ds(4, 4)
            st["r"].arrived()
            src = wbuf.at[i, c, lo, yat(-1)]
            st["rr"] = post(src, src, to_y(1), landing=wbuf.at[i, c, lo, yat(2)])
            st["l"].arrived()
            src = wbuf.at[i, c, hi, yat(1)]
            st["ll"] = post(src, src, to_y(-1), landing=wbuf.at[i, c, hi, yat(2)])
            share(yat(-1))
            share(yat(1))

        def end():
            st["rr"].arrived()
            st["ll"].arrived()
            share(yat(2))

        def ready():
            for link in sib:
                link.arrived()
        return begin, middle, end, ready

    q_begin, q_middle, q_end, q_ready = w_y(0)
    k_begin, k_middle, k_end, k_ready = w_y(1)
    v_begin, v_middle, v_end, v_ready = w_y(2)

    in_k.wait()
    in_v.wait()
    kv_step(0)
    in_kv.wait()
    wkv_step(0)

    @pl.when(wo_self)
    def _():
        wo_local.wait()

    @pl.when(jnp.logical_not(wo_self))
    def _():
        wo_first(False).wait_send()
        wo_first(True).wait_recv()

    wo_y = [post(wo_blk(z, y), wo_blk(z, y), to_y(d), landing=wo_blk(z, yat(-d))) for d in (1, 3, 2)]
    every = pl.ds(0, NY)
    lo_y, hi_y = pl.ds(0, 2), pl.ds(2, 2)
    wo_step, _ = ring(lambda b: wo_blk(b, every), lambda b: wo_blk(b, lo_y), lambda b: wo_blk(b, hi_y))

    rows_i = lax.broadcasted_iota(jnp.int32, (ROWS, HD), 0)
    lanes_i = lax.broadcasted_iota(jnp.int32, (ROWS, HD), 1)
    for s in range(16):
        limit = counts[s * NY + y]
        keep = jnp.logical_or(rows_i < limit, lanes_i > 0)
        mask[s] = jnp.where(keep, 0.0, NEG).astype(BF16)

    wkv_step(1)
    for link in wq_z:
        link.arrived()
    q_begin()
    wkv_step(2)

    @pl.when(stays)
    def _():
        tok_local.wait()

    @pl.when(jnp.logical_not(stays))
    def _():
        tok_copy(0).wait()
        tok_copy(1).wait()

    for copy in small:
        copy.wait()

    def modulate(i, carry):
        r = pl.ds(pl.multiple_of(i * 16, 16), 16)
        t = tok[r, :].astype(F32)
        mean = jnp.mean(t, axis=1, keepdims=True)
        t = t - mean
        var = jnp.mean(t * t, axis=1, keepdims=True)
        t = t * lax.rsqrt(var + 1e-6)
        xmod[r, :] = (t * (1.0 + scale[...]) + shift[...]).astype(BF16)
        return carry

    lax.fori_loop(0, ROWS // 16, modulate, 0)
    wkv_step(3)
    kv_step(1)
    q_middle()
    wkv_step(4)
    q_end()
    k_begin()
    kv_step(2)
    q_ready()

    def project(i):
        return jnp.dot(xmod[...], wbuf[i].reshape(D, HQ), preferred_element_type=F32)

    def head_norm(r):
        return r / jnp.sqrt(jnp.mean(r * r, axis=1, keepdims=True) + 1e-6)

    raw = project(0)
    for j in range(3):
        cols = slice(j * HD, (j + 1) * HD)
        qbuf[y, :, cols] = (head_norm(raw[:, cols]) * gain[...]).astype(BF16)
    q_links = {}
    for d in (1, 3, 2):
        q_links[d] = post(qbuf.at[y], qbuf.at[y], to_y(d), landing=qbuf.at[yat(-d)])
    ones = jnp.ones((768, HD), BF16)

    lane = lax.broadcasted_iota(jnp.int32, (ROWS, HD), 1)

    def absorb(j, zs, fresh_start):
        cols = pl.ds(pl.multiple_of(j * HD, HD), HD)
        q = jnp.concatenate([qbuf[y, :, cols], jnp.where(lane == 0, 1.0, 0.0).astype(BF16)], axis=1)
        places = [(cc, zz) for cc in range(2) for zz in zs]
        kb = jnp.concatenate(
            [jnp.concatenate([kv[0, cc, zz, :, cols], mask[cc * NZ + zz]], axis=1) for cc, zz in places],
            axis=0)
        s = lax.dot_general(q, kb, (((1,), (1,)), ((), ())), preferred_element_type=F32)
        top = s[:, :HD]
        for t in range(1, 6):
            top = jnp.maximum(top, s[:, t * HD:(t + 1) * HD])
        m = jnp.max(top, axis=1, keepdims=True)
        if not fresh_start:
            old = run_m[j][:, :1]
            m = jnp.maximum(m, old)
        w = jnp.exp2((s - m) * C2).astype(BF16)
        vb = jnp.concatenate([kv[1, cc, zz, :, cols] for cc, zz in places], axis=0)
        acc = jnp.dot(w, jnp.concatenate([vb, ones], axis=1), preferred_element_type=F32)
        if not fresh_start:
            acc = acc + run_acc[j] * jnp.exp2((old - m) * C2)
        run_m[j] = jnp.broadcast_to(m, (ROWS, HD))
        run_acc[j] = acc

    def absorb_all(zs, fresh_start):
        def one(j, carry):
            absorb(j, zs, fresh_start)
            return carry
        lax.fori_loop(0, 3, one, 0)

    others = (1, 3, 2)
    wide = len(others) * ROWS
    lane_w = lax.broadcasted_iota(jnp.int32, (wide, HD), 1)

    def remote_head(j):
        cols = slice(j * HD, (j + 1) * HD)
        q = jnp.concatenate([qbuf[yat(d), :, cols] for d in others], axis=0)
        q = jnp.concatenate([q, jnp.where(lane_w == 0, 1.0, 0.0).astype(BF16)], axis=1)

        def scores(b):
            cc, zz = b // 2, 4 * (b % 2)
            kb = jnp.concatenate([kv[0, cc, zz:zz + 4, :, cols].reshape(768, HD),
                                  mask[4 * b:4 * b + 4].reshape(768, HD)], axis=1)
            return lax.dot_general(q, kb, (((1,), (1,)), ((), ())), preferred_element_type=F32)

        m, acc, s = None, None, scores(0)
        for b in range(4):
            ahead = scores(b + 1) if b < 3 else None
            top = s[:, :HD]
            for t in range(1, 6):
                top = jnp.maximum(top, s[:, t * HD:(t + 1) * HD])
            new = jnp.max(top, axis=1, keepdims=True)
            if m is not None:
                new = jnp.maximum(new, m)
            w = jnp.exp2((s - new) * C2).astype(BF16)
            cc, zz = b // 2, 4 * (b % 2)
            vb = jnp.concatenate([kv[1, cc, zz:zz + 4, :, cols].reshape(768, HD), ones], axis=1)
            pv = jnp.dot(w, vb, preferred_element_type=F32)
            acc = pv if m is None else acc * jnp.exp2((m - new) * C2) + pv
            m, s = new, ahead
        total = acc[:, HD:]
        o = (acc[:, :HD] / total).astype(BF16)
        lse = m * C2 + jnp.log2(total)
        stat[...] = jnp.where(lane_w % 4 == j, lse, 0.0 if j == 0 else stat[...])
        for n, d in enumerate(others):
            osend[d, j] = o[n * ROWS:(n + 1) * ROWS]
            o_links.append(post(osend.at[d, j], orecv.at[d, j], to_y(d)))
        if j == 2:
            full = stat[...]
            top = full.astype(BF16).astype(F32)
            mid = (full - top).astype(BF16).astype(F32)
            low = full - top - mid
            packed = jnp.where(lane_w < 4, top, jnp.where(lane_w < 8, mid, low)).astype(BF16)
            for n, d in enumerate(others):
                osend[d, 3] = packed[n * ROWS:(n + 1) * ROWS]
                o_links.append(post(osend.at[d, 3], orecv.at[d, 3], to_y(d)))

    o_links = []
    kv_sib[1].arrived()
    kv_sib[2].arrived()
    absorb_all((zat(-1), zat(1)), True)
    kv_step(3)
    kv_sib[3].arrived()
    kv_sib[4].arrived()
    absorb_all((zat(-2), zat(2)), False)
    kv_step(4)
    for link in wo_y:
        link.arrived()
    wo_step(0)
    k_middle()
    v_begin()
    kv_sib[5].arrived()
    kv_sib[6].arrived()
    absorb_all((zat(-3), zat(3)), False)
    kv_sib[0].arrived()
    kv_sib[7].arrived()
    for link in q_links.values():
        link.arrived()
    remote_head(0)
    k_end()
    v_middle()
    wo_step(1)
    remote_head(1)
    v_end()
    wo_step(2)
    remote_head(2)
    k_ready()
    raw = project(1)
    for j in range(3):
        cols = slice(j * HD, (j + 1) * HD)
        mix[:, cols] = head_norm(raw[:, cols]).astype(BF16)
    wo_step(3)
    v_ready()
    mix[:, HQ:] = project(2).astype(BF16)

    for link in kv_state[0] + (kv_sib[0],):
        link.done()
    kv[0, c, z] = mix[:, :HQ]
    kv[1, c, z] = mix[:, HQ:]
    wo_step(4)
    blk = wo.at[pl.ds(2 * c, 2)]
    wo_s = post(blk, blk, sibling, landing=wo.at[pl.ds(2 * oc, 2)])

    for j in range(3):
        absorb(j, (z, zat(4)), False)
    for link in o_links:
        link.arrived()
    att_links = []
    for j in range(3):
        cols = slice(j * HD, (j + 1) * HD)
        total = run_acc[j][:, HD:]
        parts = [run_acc[j][:, :HD] / total]
        lses = [run_m[j][:, :1] * C2 + jnp.log2(total[:, :1])]
        for d in (1, 3, 2):
            parts.append(orecv[d, j].astype(F32))
            st = jnp.where(jnp.logical_and(lane % 4 == j, lane < 12), orecv[d, 3].astype(F32), 0.0)
            lses.append(jnp.sum(st, axis=1, keepdims=True))
        top = functools.reduce(jnp.maximum, lses)
        ws = [jnp.exp2(v - top) for v in lses]
        total = functools.reduce(jnp.add, ws)
        mixd = functools.reduce(jnp.add, [w * o for w, o in zip(ws, parts)])
        att[x, :, cols] = (mixd / total).astype(BF16)
        for k in (1, 3, 2):
            att_links.append(post(att.at[x, :, pl.ds(j * HD, HD)], att.at[x, :, pl.ds(j * HD, HD)],
                                  dev(xat(k), z, y, c),
                                  landing=att.at[xat(-k), :, pl.ds(j * HD, HD)]))
    wo_s.arrived()
    in_g.wait()
    for link in att_links:
        link.arrived()
    last = []
    for n in range(3):
        acc = jnp.zeros((ROWS, 256), F32)
        for g in range(NX):
            wt = wo[g].reshape(768, HQ)[n * 256:(n + 1) * 256]
            acc = acc + lax.dot_general(att[g], wt, (((1,), (1,)), ((), ())),
                                        preferred_element_type=F32)
        cols = slice(n * 256, (n + 1) * 256)
        mix[:, cols] = (acc * gbuf[:, cols]).astype(BF16)
        part = pl.ds(n * 256, 256)
        last.append(Swap(mix.at[:, part], out.at[:, part], out.at[:, part]).start())
    for swap in last:
        swap.wait()
    for link in links:
        link.done()
    assert next_sem[0] <= N_SEM, next_sem[0]


def shards(tokens, valid_counts, mod_shift, mod_scale, mod_gate, q_gain, w_qkv, w_out,
           stale_keys, stale_values):
    hbm = pl.BlockSpec(memory_space=pltpu.HBM)
    return pl.pallas_call(
        kernel,
        out_shape=jax.ShapeDtypeStruct((ROWS, 768), BF16),
        in_specs=[pl.BlockSpec(memory_space=pltpu.SMEM)] + [hbm] * 9,
        out_specs=hbm,
        scratch_shapes=[
            pltpu.VMEM((ROWS, D), BF16),
            pltpu.VMEM((1, D), F32),
            pltpu.VMEM((1, D), F32),
            pltpu.VMEM((1, HD), F32),
            pltpu.VMEM((ROWS, D), BF16),
            pltpu.VMEM((3, 2, NZ, NY, SHARD, HQ), BF16),
            pltpu.VMEM((2, 2, NZ, ROWS, HQ), BF16),
            pltpu.VMEM((16, ROWS, HD), BF16),
            pltpu.VMEM((NY, ROWS, HQ), BF16),
            pltpu.VMEM((3 * ROWS, HD), F32),
            pltpu.VMEM((NY, 4, ROWS, HD), BF16),
            pltpu.VMEM((NY, 4, ROWS, HD), BF16),
            pltpu.VMEM((NX, ROWS, HQ), BF16),
            pltpu.VMEM((4, 4, NY, SHARD, HQ), BF16),
            pltpu.VMEM((1, 768), F32),
            pltpu.VMEM((ROWS, 768), BF16),
            pltpu.VMEM((3, ROWS, HD), F32),
            pltpu.VMEM((3, ROWS, 2 * HD), F32),
            pltpu.SemaphoreType.DMA((N_SEM,)),
            pltpu.SemaphoreType.DMA((N_SEM,)),
        ],
        compiler_params=pltpu.CompilerParams(
            collective_id=0, has_side_effects=True, vmem_limit_bytes=63 * 2**20),
    )(valid_counts, tokens, mod_scale.reshape(1, D), mod_shift.reshape(1, D),
      q_gain.reshape(1, HD), mod_gate.reshape(1, 768), jnp.transpose(w_qkv, (1, 0, 2)),
      jnp.transpose(w_out), stale_keys, stale_values)


def solution(mesh):
    in_specs = (
        P("patch", None), P(), P(), P(), P("head"), P(), P("patch", None, "head"),
        P("head", "patch"), P("patch", "head"), P("patch", "head"),
    )
    return jax.shard_map(shards, mesh=mesh, in_specs=in_specs, out_specs=P("patch", "head"),
                         check_vma=False)
```

time: 116 us -> 107 us (0.922)
  local copies, waits for them, and re-layouts: 8.88 us -> 2.96 us
  Pallas kernels: 107 us -> 104 us
    unnamed x19 -> x1, local copies, waits for them, and re-layouts: 8.19 us -> 1.69 us
    pallas_call x1, Pallas kernels: 107 us -> 104 us  [shards(): pl.pallas_call(kernel, out_shape=jax.ShapeDtypeStruct((ROWS, 768), BF16),...]
where the time goes in v2:
time: 107 us
  Pallas kernels  104 us (97%)
  local copies, waits for them, and re-layouts  2.96 us (3%)
    pallas_call x1, Pallas kernels, shards(): pl.pallas_call(kernel, out_shape=jax.ShapeDtypeStruct((ROWS, 768), BF16),...  104 us

profile of v2, /device:TPU:1, one launch (start us, length us, event | category | flops | bytes accessed | tf_op | source)
XLA Modules:
  0.0 107.0 jit_solution(5559476045140222505)
XLA Ops:
  0.0 1.3 %reshape.15.gate = f32[1,768]{1,0:T(1,128)} reshape(f32[768]{0:T(1024)} %param.14) | data formatting | bytes 6144 | tf_op jit(solution)/shard_map/reshape | solution.py:569
  1.3 104.0 %shard_map.100 = bf16[192,768]{1,0:T(8,128)(2,1)} custom-call(s32[64]{0:T(128)} %counts.1, bf16[192,3072]{1,0:T(8,128)(2,1)} %tokens.1, f32[1,3072]{1,0:T(1,128)} %bitcast.7, f32[1,3072]{1,0:T(1,128)} %bitcast.8, f32[1,128]{1,0:T(1,128)} %bitcast.9, f32[1,768]{1,0:T(1,128)} %reshape.15.gate, bf16[3,48,384]{2,1,0:T(8,128)(2,1)} %bitcast.5, ...), custom_call_target="tpu_custom_call" | custom-call | tf_op jit(solution)/shard_map/pallas_call | solution.py:539
  105.3 1.7 %copy.12 = bf16[192,768]{1,0:T(8,128)(2,1)} copy(bf16[192,768]{1,0:T(8,128)(2,1)} %shard_map.100) | data formatting | bytes 589824

commit v3 on v2

--- a/solution.py
+++ b/solution.py
@@ -19,7 +19,7 @@
 SHARD = 48
 C2 = math.log2(math.e) / math.sqrt(HD)
 NEG = -1e30
-N_SEM = 112
+N_SEM = 168
 
 
 def dev(x, z, y, c):
@@ -157,8 +157,8 @@
     wo_self = jnp.logical_and(jnp.logical_and(wo_x == x, wo_c == c), c == 0)
     wo_sem = new_sem()
 
-    def wo_blk(zz, ys):
-        group = 2 * c + jnp.where(zz // 4 == xl, 0, 1)
+    def wo_blk(zz, ys, cc=c):
+        group = 2 * cc + jnp.where(zz // 4 == xl, 0, 1)
         return wo.at[group, lax.rem(zz, 4), ys]
 
     def wo_first(landing):
@@ -224,49 +224,65 @@
             state[s] = (right, left)
         return step, state
 
-    wkv_step, _ = ring(lambda b: wbuf.at[pl.ds(1, 2), c, b, y],
-                    lambda b: wbuf.at[pl.ds(1, 1), c, b, y],
-                    lambda b: wbuf.at[pl.ds(2, 1), c, b, y])
-    kv_ring, kv_state = ring(lambda b: kv.at[:, c, b],
-                   lambda b: kv.at[pl.ds(0, 1), c, b],
-                   lambda b: kv.at[pl.ds(1, 1), c, b])
-    kv_sib = []
-
-    def kv_share(b):
-        kv_sib.append(post(kv.at[:, c, b], kv.at[:, c, b], sibling, landing=kv.at[:, oc, b]))
+    def shared_ring(block, first, second):
+        hop, state = ring(lambda b: block(b, c), first, second)
+        shares = []
+
+        def share(b):
+            shares.append(post(block(b, c), block(b, c), sibling, landing=block(b, oc)))
+
+        def step(s):
+            hop(s)
+            if s == 0:
+                share(z)
+            elif s < 4:
+                share(zat(-s))
+                share(zat(s))
+            else:
+                share(zat(4))
+        return step, state, shares
+
+    wk_step, _ = ring(lambda b: wbuf.at[1, c, b, y], lambda b: wbuf.at[1, c, b, y, pl.ds(0, 16)],
+                      lambda b: wbuf.at[1, c, b, y, pl.ds(16, 32)])
+    upper, lower = pl.ds(0, ROWS // 2), pl.ds(ROWS // 2, ROWS // 2)
+    key_step, key_state, key_sib = shared_ring(
+        lambda b, cc: kv.at[0, cc, b], lambda b: kv.at[0, c, b, upper], lambda b: kv.at[0, c, b, lower])
+    val_step, val_state, val_sib = shared_ring(
+        lambda b, cc: kv.at[1, cc, b], lambda b: kv.at[1, c, b, upper], lambda b: kv.at[1, c, b, lower])
 
     def kv_step(s):
-        kv_ring(s)
-        if s == 0:
-            kv_share(z)
-        elif s < 4:
-            kv_share(zat(-s))
-            kv_share(zat(s))
-        else:
-            kv_share(zat(4))
-
-    def w_y(i):
+        key_step(s)
+        val_step(s)
+
+    def kv_wait(*which):
+        for i in which:
+            key_sib[i].arrived()
+            val_sib[i].arrived()
+
+    lo_y, hi_y = pl.ds(0, 2), pl.ds(2, 2)
+    wv_step, _, wv_sib = shared_ring(
+        lambda b, cc: wbuf.at[2, cc, b], lambda b: wbuf.at[2, c, b, lo_y], lambda b: wbuf.at[2, c, b, hi_y])
+    wo_step, _ = ring(lambda b: wo_blk(b, y), lambda b: wo_blk(b, y).at[pl.ds(0, 16)],
+                      lambda b: wo_blk(b, y).at[pl.ds(16, 32)])
+
+    def round_y(block, low, high):
         st = {}
         sib = []
 
         def share(b):
-            sib.append(post(wbuf.at[i, c, :, b], wbuf.at[i, c, :, b], sibling,
-                            landing=wbuf.at[i, oc, :, b]))
+            sib.append(post(block(c, b), block(c, b), sibling, landing=block(oc, b)))
 
         def begin():
-            src = wbuf.at[i, c, :, y]
-            st["r"] = post(src, src, to_y(1), landing=wbuf.at[i, c, :, yat(-1)])
-            st["l"] = post(src, src, to_y(-1), landing=wbuf.at[i, c, :, yat(1)])
+            src = block(c, y)
+            st["r"] = post(src, src, to_y(1), landing=block(c, yat(-1)))
+            st["l"] = post(src, src, to_y(-1), landing=block(c, yat(1)))
             share(y)
 
         def middle():
-            lo, hi = pl.ds(0, 4), pl.ds(4, 4)
             st["r"].arrived()
-            src = wbuf.at[i, c, lo, yat(-1)]
-            st["rr"] = post(src, src, to_y(1), landing=wbuf.at[i, c, lo, yat(2)])
+            st["rr"] = post(low(yat(-1)), low(yat(-1)), to_y(1), landing=low(yat(2)))
             st["l"].arrived()
-            src = wbuf.at[i, c, hi, yat(1)]
-            st["ll"] = post(src, src, to_y(-1), landing=wbuf.at[i, c, hi, yat(2)])
+            st["ll"] = post(high(yat(1)), high(yat(1)), to_y(-1), landing=high(yat(2)))
             share(yat(-1))
             share(yat(1))
 
@@ -280,15 +296,21 @@
                 link.arrived()
         return begin, middle, end, ready
 
+    def w_y(i):
+        return round_y(lambda cc, b: wbuf.at[i, cc, :, b], lambda b: wbuf.at[i, c, pl.ds(0, 4), b],
+                       lambda b: wbuf.at[i, c, pl.ds(4, 4), b])
+
+    wo_rows = pl.ds(2 * c, 2)
+    wo_begin, wo_middle, wo_end, wo_ready = round_y(
+        lambda cc, b: wo.at[pl.ds(2 * cc, 2), :, b], lambda b: wo.at[wo_rows, pl.ds(0, 2), b],
+        lambda b: wo.at[wo_rows, pl.ds(2, 2), b])
     q_begin, q_middle, q_end, q_ready = w_y(0)
     k_begin, k_middle, k_end, k_ready = w_y(1)
-    v_begin, v_middle, v_end, v_ready = w_y(2)
-
-    in_k.wait()
-    in_v.wait()
-    kv_step(0)
+
     in_kv.wait()
-    wkv_step(0)
+    wk_step(0)
+    wv_y = [post(wbuf.at[2, c, z, y], wbuf.at[2, c, z, y], to_y(d), landing=wbuf.at[2, c, z, yat(-d)])
+            for d in (1, 3, 2)]
 
     @pl.when(wo_self)
     def _():
@@ -299,10 +321,7 @@
         wo_first(False).wait_send()
         wo_first(True).wait_recv()
 
-    wo_y = [post(wo_blk(z, y), wo_blk(z, y), to_y(d), landing=wo_blk(z, yat(-d))) for d in (1, 3, 2)]
-    every = pl.ds(0, NY)
-    lo_y, hi_y = pl.ds(0, 2), pl.ds(2, 2)
-    wo_step, _ = ring(lambda b: wo_blk(b, every), lambda b: wo_blk(b, lo_y), lambda b: wo_blk(b, hi_y))
+    wo_step(0)
 
     rows_i = lax.broadcasted_iota(jnp.int32, (ROWS, HD), 0)
     lanes_i = lax.broadcasted_iota(jnp.int32, (ROWS, HD), 1)
@@ -311,11 +330,16 @@
         keep = jnp.logical_or(rows_i < limit, lanes_i > 0)
         mask[s] = jnp.where(keep, 0.0, NEG).astype(BF16)
 
-    wkv_step(1)
+    wk_step(1)
+    wo_step(1)
+    in_k.wait()
+    in_v.wait()
     for link in wq_z:
         link.arrived()
     q_begin()
-    wkv_step(2)
+    kv_step(0)
+    wk_step(2)
+    wo_step(2)
 
     @pl.when(stays)
     def _():
@@ -340,14 +364,15 @@
         return carry
 
     lax.fori_loop(0, ROWS // 16, modulate, 0)
-    wkv_step(3)
+    wk_step(3)
+    wo_step(3)
+    q_middle()
+    wk_step(4)
     kv_step(1)
-    q_middle()
-    wkv_step(4)
     q_end()
     k_begin()
+    q_ready()
     kv_step(2)
-    q_ready()
 
     def project(i):
         return jnp.dot(xmod[...], wbuf[i].reshape(D, HQ), preferred_element_type=F32)
@@ -443,50 +468,46 @@
                 o_links.append(post(osend.at[d, 3], orecv.at[d, 3], to_y(d)))
 
     o_links = []
-    kv_sib[1].arrived()
-    kv_sib[2].arrived()
+    kv_wait(1, 2)
     absorb_all((zat(-1), zat(1)), True)
+    kv_wait(3, 4)
+    absorb_all((zat(-2), zat(2)), False)
     kv_step(3)
-    kv_sib[3].arrived()
-    kv_sib[4].arrived()
-    absorb_all((zat(-2), zat(2)), False)
+    for link in wv_y:
+        link.arrived()
+    wv_step(0)
+    k_middle()
+    wo_step(4)
+    wo_begin()
+    kv_wait(5, 6)
+    absorb_all((zat(-3), zat(3)), False)
     kv_step(4)
-    for link in wo_y:
-        link.arrived()
-    wo_step(0)
-    k_middle()
-    v_begin()
-    kv_sib[5].arrived()
-    kv_sib[6].arrived()
-    absorb_all((zat(-3), zat(3)), False)
-    kv_sib[0].arrived()
-    kv_sib[7].arrived()
+    wv_step(1)
+    kv_wait(0, 7)
     for link in q_links.values():
         link.arrived()
     remote_head(0)
     k_end()
-    v_middle()
-    wo_step(1)
+    wv_step(2)
+    wo_middle()
     remote_head(1)
-    v_end()
-    wo_step(2)
+    wv_step(3)
+    wo_end()
     remote_head(2)
+    wv_step(4)
     k_ready()
     raw = project(1)
     for j in range(3):
         cols = slice(j * HD, (j + 1) * HD)
         mix[:, cols] = head_norm(raw[:, cols]).astype(BF16)
-    wo_step(3)
-    v_ready()
+    for link in wv_sib:
+        link.arrived()
     mix[:, HQ:] = project(2).astype(BF16)
 
-    for link in kv_state[0] + (kv_sib[0],):
+    for link in key_state[0] + val_state[0] + (key_sib[0], val_sib[0]):
         link.done()
     kv[0, c, z] = mix[:, :HQ]
     kv[1, c, z] = mix[:, HQ:]
-    wo_step(4)
-    blk = wo.at[pl.ds(2 * c, 2)]
-    wo_s = post(blk, blk, sibling, landing=wo.at[pl.ds(2 * oc, 2)])
 
     for j in range(3):
         absorb(j, (z, zat(4)), False)
@@ -511,7 +532,7 @@
             att_links.append(post(att.at[x, :, pl.ds(j * HD, HD)], att.at[x, :, pl.ds(j * HD, HD)],
                                   dev(xat(k), z, y, c),
                                   landing=att.at[xat(-k), :, pl.ds(j * HD, HD)]))
-    wo_s.arrived()
+    wo_ready()
     in_g.wait()
     for link in att_links:
         link.arrived()

time: 107 us -> 98.1 us (0.917)
  Pallas kernels: 104 us -> 95 us
    pallas_call x1, Pallas kernels: 104 us -> 95 us  [shards(): pl.pallas_call(kernel, out_shape=jax.ShapeDtypeStruct((ROWS, 768), BF16),...]
where the time goes in v3:
time: 98.1 us; the launch traced here: 98 us
  Pallas kernels  95 us (97%)
  local copies, waits for them, and re-layouts  2.96 us (3%)
    pallas_call x1, Pallas kernels, shards(): pl.pallas_call(kernel, out_shape=jax.ShapeDtypeStruct((ROWS, 768), BF16),...  95 us

profile of v3, /device:TPU:1, one launch (start us, length us, event | category | flops | bytes accessed | tf_op | source)
XLA Modules:
  0.0 98.0 jit_solution(18067564526227584178)
XLA Ops:
  0.0 1.3 %reshape.15.gate = f32[1,768]{1,0:T(1,128)} reshape(f32[768]{0:T(1024)} %param.14) | data formatting | bytes 6144 | tf_op jit(solution)/shard_map/reshape | solution.py:590
  1.3 95.0 %shard_map.100 = bf16[192,768]{1,0:T(8,128)(2,1)} custom-call(s32[64]{0:T(128)} %counts.1, bf16[192,3072]{1,0:T(8,128)(2,1)} %tokens.1, f32[1,3072]{1,0:T(1,128)} %bitcast.7, f32[1,3072]{1,0:T(1,128)} %bitcast.8, f32[1,128]{1,0:T(1,128)} %bitcast.9, f32[1,768]{1,0:T(1,128)} %reshape.15.gate, bf16[3,48,384]{2,1,0:T(8,128)(2,1)} %bitcast.5, ...), custom_call_target="tpu_custom_call" | custom-call | tf_op jit(solution)/shard_map/pallas_call | solution.py:560
  96.3 1.7 %copy.12 = bf16[192,768]{1,0:T(8,128)(2,1)} copy(bf16[192,768]{1,0:T(8,128)(2,1)} %shard_map.100) | data formatting | bytes 589824

commit v4 on v3

--- a/solution.py
+++ b/solution.py
@@ -470,15 +470,15 @@
     o_links = []
     kv_wait(1, 2)
     absorb_all((zat(-1), zat(1)), True)
+    k_middle()
+    wo_step(4)
+    wo_begin()
     kv_wait(3, 4)
     absorb_all((zat(-2), zat(2)), False)
     kv_step(3)
     for link in wv_y:
         link.arrived()
     wv_step(0)
-    k_middle()
-    wo_step(4)
-    wo_begin()
     kv_wait(5, 6)
     absorb_all((zat(-3), zat(3)), False)
     kv_step(4)
@@ -509,13 +509,13 @@
     kv[0, c, z] = mix[:, :HQ]
     kv[1, c, z] = mix[:, HQ:]
 
-    for j in range(3):
-        absorb(j, (z, zat(4)), False)
-    for link in o_links:
-        link.arrived()
     att_links = []
     for j in range(3):
         cols = slice(j * HD, (j + 1) * HD)
+        absorb(j, (z, zat(4)), False)
+        if j == 0:
+            for link in o_links:
+                link.arrived()
         total = run_acc[j][:, HD:]
         parts = [run_acc[j][:, :HD] / total]
         lses = [run_m[j][:, :1] * C2 + jnp.log2(total[:, :1])]
@@ -544,7 +544,7 @@
             acc = acc + lax.dot_general(att[g], wt, (((1,), (1,)), ((), ())),
                                         preferred_element_type=F32)
         cols = slice(n * 256, (n + 1) * 256)
-        mix[:, cols] = (acc * gbuf[:, cols]).astype(BF16)
+        mix[:, cols] = (acc * gbuf[cols].reshape(1, 256)).astype(BF16)
         part = pl.ds(n * 256, 256)
         last.append(Swap(mix.at[:, part], out.at[:, part], out.at[:, part]).start())
     for swap in last:
@@ -577,7 +577,7 @@
             pltpu.VMEM((NY, 4, ROWS, HD), BF16),
             pltpu.VMEM((NX, ROWS, HQ), BF16),
             pltpu.VMEM((4, 4, NY, SHARD, HQ), BF16),
-            pltpu.VMEM((1, 768), F32),
+            pltpu.VMEM((768,), F32),
             pltpu.VMEM((ROWS, 768), BF16),
             pltpu.VMEM((3, ROWS, HD), F32),
             pltpu.VMEM((3, ROWS, 2 * HD), F32),
@@ -587,7 +587,7 @@
         compiler_params=pltpu.CompilerParams(
             collective_id=0, has_side_effects=True, vmem_limit_bytes=63 * 2**20),
     )(valid_counts, tokens, mod_scale.reshape(1, D), mod_shift.reshape(1, D),
-      q_gain.reshape(1, HD), mod_gate.reshape(1, 768), jnp.transpose(w_qkv, (1, 0, 2)),
+      q_gain.reshape(1, HD), mod_gate, jnp.transpose(w_qkv, (1, 0, 2)),
       jnp.transpose(w_out), stale_keys, stale_values)
 
 

time: 98.1 us -> 95.6 us (0.975)
  local copies, waits for them, and re-layouts: 2.96 us -> 1.69 us
  Pallas kernels: 95 us -> 93.8 us
    reshape x1 -> x0, local copies, waits for them, and re-layouts: 1.27 us -> none  [shards(): mod_gate.reshape(1, 768)]
    pallas_call x1, Pallas kernels: 95 us -> 93.8 us  [shards(): pl.pallas_call(kernel, out_shape=jax.ShapeDtypeStruct((ROWS, 768), BF16),...]
where the time goes in v4:
time: 95.6 us; the launch traced here: 95.5 us
  Pallas kernels  93.8 us (98%)
  local copies, waits for them, and re-layouts  1.69 us (2%)
    pallas_call x1, Pallas kernels, shards(): pl.pallas_call(kernel, out_shape=jax.ShapeDtypeStruct((ROWS, 768), BF16),...  93.8 us

profile of v4, /device:TPU:1, one launch (start us, length us, event | category | flops | bytes accessed | tf_op | source)
XLA Modules:
  0.0 95.5 jit_solution(7027482594252124406)
XLA Ops:
  0.0 93.8 %shard_map.100 = bf16[192,768]{1,0:T(8,128)(2,1)} custom-call(s32[64]{0:T(128)} %counts.1, bf16[192,3072]{1,0:T(8,128)(2,1)} %tokens.1, f32[1,3072]{1,0:T(1,128)} %bitcast.7, f32[1,3072]{1,0:T(1,128)} %bitcast.8, f32[1,128]{1,0:T(1,128)} %bitcast.9, f32[768]{0:T(1024)} %gate.1, bf16[3,48,384]{2,1,0:T(8,128)(2,1)} %bitcast.5, bf16[48,384]{1,0:T(8,128)(2,1)} %bitcast.6, ...), custom_call_target="tpu_custom_call" | custom-call | tf_op jit(solution)/shard_map/pallas_call | solution.py:560
  93.8 1.7 %copy.12 = bf16[192,768]{1,0:T(8,128)(2,1)} copy(bf16[192,768]{1,0:T(8,128)(2,1)} %shard_map.100) | data formatting | bytes 589824

commit v5 on v4

--- a/solution.py
+++ b/solution.py
@@ -112,6 +112,13 @@
     @pl.when(z // 4 != xl)
     def _():
         pl.semaphore_signal(barrier, inc=1, device_id=dev(2 * c + xh, zat(4), y, 1), device_id_type=MESH)
+
+    rows_i = lax.broadcasted_iota(jnp.int32, (ROWS, HD), 0)
+    lanes_i = lax.broadcasted_iota(jnp.int32, (ROWS, HD), 1)
+    for s in range(16):
+        limit = counts[s * NY + y]
+        keep = jnp.logical_or(rows_i < limit, lanes_i > 0)
+        mask[s] = jnp.where(keep, 0.0, NEG).astype(BF16)
 
     pl.semaphore_wait(barrier, 2 * NX - 1 + NZ - 1 + NY - 1 + c)
 
@@ -323,21 +330,14 @@
 
     wo_step(0)
 
-    rows_i = lax.broadcasted_iota(jnp.int32, (ROWS, HD), 0)
-    lanes_i = lax.broadcasted_iota(jnp.int32, (ROWS, HD), 1)
-    for s in range(16):
-        limit = counts[s * NY + y]
-        keep = jnp.logical_or(rows_i < limit, lanes_i > 0)
-        mask[s] = jnp.where(keep, 0.0, NEG).astype(BF16)
-
     wk_step(1)
     wo_step(1)
     in_k.wait()
     in_v.wait()
+    kv_step(0)
     for link in wq_z:
         link.arrived()
     q_begin()
-    kv_step(0)
     wk_step(2)
     wo_step(2)
 

time: 95.6 us -> 95.6 us (level)
  no operation moved by 1% of the time
where the time goes in v5:
time: 95.6 us; the launch traced here: 95.5 us
  Pallas kernels  93.8 us (98%)
  local copies, waits for them, and re-layouts  1.69 us (2%)
    pallas_call x1, Pallas kernels, shards(): pl.pallas_call(kernel, out_shape=jax.ShapeDtypeStruct((ROWS, 768), BF16),...  93.8 us

profile of v5, /device:TPU:1, one launch (start us, length us, event | category | flops | bytes accessed | tf_op | source)
XLA Modules:
  0.0 95.5 jit_solution(1122824370620346547)
XLA Ops:
  0.0 93.8 %shard_map.100 = bf16[192,768]{1,0:T(8,128)(2,1)} custom-call(s32[64]{0:T(128)} %counts.1, bf16[192,3072]{1,0:T(8,128)(2,1)} %tokens.1, f32[1,3072]{1,0:T(1,128)} %bitcast.7, f32[1,3072]{1,0:T(1,128)} %bitcast.8, f32[1,128]{1,0:T(1,128)} %bitcast.9, f32[768]{0:T(1024)} %gate.1, bf16[3,48,384]{2,1,0:T(8,128)(2,1)} %bitcast.5, bf16[48,384]{1,0:T(8,128)(2,1)} %bitcast.6, ...), custom_call_target="tpu_custom_call" | custom-call | tf_op jit(solution)/shard_map/pallas_call | solution.py:560
  93.8 1.7 %copy.12 = bf16[192,768]{1,0:T(8,128)(2,1)} copy(bf16[192,768]{1,0:T(8,128)(2,1)} %shard_map.100) | data formatting | bytes 589824
